TPU v7x, 32 devices: a whole 2x2x4 slice. The times are simulated.
32 devices in a mesh: row: 4 (over y, x), col: 8 (over z, core).
Axes of the slice: x: 2, y: 2, z: 4, core: 2. Of those that a mesh axis runs over, the one named last changes fastest.
Arguments:
- features: bfloat16 [16384, 256], P(('col', 'row')), may hold values from -6 to 6
- weight: bfloat16 [256, 256], replicated, may hold values from -0.375 to 0.375
- bias: float32 [256], replicated, may hold values from -4 to 4
- cotangent: bfloat16 [16384, 256], P(('row', 'col')), may hold values from -6 to 6
- tiles: bfloat16 [4, 8, 384, 128, 128], P('row', 'col'), may hold values from -0.0546875 to 0.0546875
- tile_rows: int32 [4, 8, 384], P('row', 'col'), may hold values from 0 to 31, as said below
- tile_cols: int32 [4, 8, 384], P('row', 'col'), may hold values from 0 to 15
- tile_counts: int32 [4, 8], P('row', 'col'), may hold values from 24 to 384, as said below
Outputs:
- hidden: bfloat16 [16384, 256], P(('row', 'col'))
- grad_weight: float32 [256, 256], replicated
- grad_bias: float32 [256], replicated
- grad_features: bfloat16 [16384, 256], P(('col', 'row'))
Inputs may be any that keep to these rules, and one draw needn't show every extreme that they name: `tile_rows`: on each grid cell the slots name distinct blocks. `tile_counts`: slots at or after a cell's count are unused; some cell uses all 384 slots.
All inputs are finite; a program needn't handle non-finite values.
Results may differ from a plain program's by a relative error of at most 0.013.
Values may be sent and summed in bfloat16 or wider, within the bound.
No kernel may reach another device: no remote copies, remote signals or barrier semaphores. Data moves between devices by JAX's collectives and lax.ppermute only.
A program may use at most 128 MiB of HBM per device.

v0:
```python
import math

import jax
import jax.numpy as jnp
from jax import lax
from jax.sharding import PartitionSpec as P


def accumulate(tiles, dest_ids, source_ids, live_count, source_blocks, out_blocks, backward):
    slots = tiles.shape[0]
    group = math.gcd(slots, 32)
    block = tiles.shape[-1]
    width = source_blocks.shape[-1]
    in_blocks = source_blocks.shape[0]
    flat_source = source_blocks.reshape(in_blocks, block * width)
    in_range = jnp.arange(in_blocks, dtype=jnp.int32)
    out_range = jnp.arange(out_blocks, dtype=jnp.int32)

    def one_group(step_index, total):
        start = step_index * group
        tile_group = lax.dynamic_slice_in_dim(tiles, start, group, 0)
        dest_group = lax.dynamic_slice_in_dim(dest_ids, start, group, 0)
        source_group = lax.dynamic_slice_in_dim(source_ids, start, group, 0)
        live = start + jnp.arange(group, dtype=jnp.int32) < live_count
        if backward:
            fetch_ids = dest_group
            target = source_group
        else:
            fetch_ids = source_group
            target = dest_group
        picker = (fetch_ids[:, None] == in_range[None, :]).astype(jnp.bfloat16)
        fetched = jnp.dot(picker, flat_source, preferred_element_type=jnp.float32)
        fetched = fetched.astype(jnp.bfloat16).reshape(group, block, width)
        if backward:
            contrib = jnp.einsum(
                "tji,tjf->tif", tile_group, fetched, preferred_element_type=jnp.float32
            )
        else:
            contrib = jnp.einsum(
                "tij,tjf->tif", tile_group, fetched, preferred_element_type=jnp.float32
            )
        placer = ((target[:, None] == out_range[None, :]) & live[:, None]).astype(jnp.float32)
        added = jnp.dot(
            placer.T,
            contrib.reshape(group, block * width),
            precision=lax.Precision.HIGHEST,
            preferred_element_type=jnp.float32,
        )
        return total + added

    start_total = jnp.zeros((out_blocks, block * width), jnp.float32)
    result = lax.fori_loop(0, slots // group, one_group, start_total)
    return result.reshape(out_blocks, block, width)


def per_device(features, weight, bias, cotangent, tiles, tile_rows, tile_cols, tile_counts):
    tile_set = tiles[0, 0]
    dest_ids = tile_rows[0, 0]
    source_ids = tile_cols[0, 0]
    live_count = tile_counts[0, 0]
    block = tile_set.shape[-1]
    own_nodes = features.shape[0]
    width = features.shape[1]
    row_count = lax.axis_size("row")
    col_count = lax.axis_size("col")
    blocks_down = own_nodes * col_count // block
    blocks_across = own_nodes * row_count // block
    factor = 1.0 / math.sqrt(own_nodes * row_count * col_count)
    panel = lax.all_gather(features, "row", axis=0, tiled=True)
    panel_blocks = panel.reshape(blocks_across, block, width)
    partial_value = accumulate(
        tile_set, dest_ids, source_ids, live_count, panel_blocks, blocks_down, False
    )
    term = partial_value.reshape(blocks_down * block, width)
    summed = lax.psum_scatter(term, "col", scatter_dimension=0, tiled=True)
    aggregated = summed.astype(jnp.bfloat16)
    preact = jnp.dot(aggregated, weight, preferred_element_type=jnp.float32) + bias
    hidden = jax.nn.silu(preact).astype(jnp.bfloat16)
    sigma = jax.nn.sigmoid(preact)
    slope = sigma * (1.0 + preact * (1.0 - sigma))
    grad_pre = (cotangent.astype(jnp.float32) * slope).astype(jnp.bfloat16)
    local_weight = jnp.einsum("nf,ng->fg", aggregated, grad_pre, preferred_element_type=jnp.float32)
    local_bias = jnp.sum(grad_pre.astype(jnp.float32), axis=0)
    grad_agg = jnp.dot(grad_pre, weight.T, preferred_element_type=jnp.float32).astype(jnp.bfloat16)
    grad_panel = lax.all_gather(grad_agg, "col", axis=0, tiled=True)
    grad_blocks = grad_panel.reshape(blocks_down, block, width)
    partial_back = accumulate(
        tile_set, dest_ids, source_ids, live_count, grad_blocks, blocks_across, True
    )
    term_back = partial_back.reshape(blocks_across * block, width)
    grad_features = lax.psum_scatter(
        term_back.astype(jnp.bfloat16), "row", scatter_dimension=0, tiled=True
    )
    grad_weight, grad_bias = lax.psum((local_weight, local_bias), ("row", "col"))
    grad_weight = grad_weight * factor
    grad_bias = grad_bias * factor
    return (hidden, grad_weight, grad_bias, grad_features)


def solution(mesh):
    in_specs = (
        P(("col", "row"), None),
        P(),
        P(),
        P(("row", "col"), None),
        P("row", "col", None, None, None),
        P("row", "col", None),
        P("row", "col", None),
        P("row", "col"),
    )
    out_specs = (P(("row", "col"), None), P(), P(), P(("col", "row"), None))
    return jax.shard_map(
        per_device, mesh=mesh, in_specs=in_specs, out_specs=out_specs, check_vma=False
    )
```

profile of v0, /device:TPU:0, one launch (start us, length us, event | category | flops | bytes accessed | tf_op | source)
XLA Modules:
  0.0 537.7 jit_solution(8601466751281304663)
XLA Ops:
  9.4 29.8 %all-gather.3.cloned.1.call-done = bf16[2048,256]{1,0:T(8,128)(2,1)} async-done(((bf16[512,256]{1,0:T(8,128)(2,1)}), bf16[2048,256]{1,0:T(8,128)(2,1)}) %all-gather.3.cloned.1.call-update) | async-done | bytes 1048592 | tf_op jit(solution)/shard_map/all_gather | solution.py:69
  40.8 193.0 %while.28 = (s32[]{:T(128)}, f32[32,32768]{1,0:T(8,128)}, s32[384]{0:T(512)S(1)}, s32[]{:T(128)}, bf16[384,128,128]{2,1,0:T(8,128)(2,1)}, /*index=5*/s32[384]{0:...) while((s32[]{:T(128)}, f32[32,32768]{1,0:T(8,128)}, ...), condition=%wide.region_1.0_spmd.clone, body=%wide.region_0.0_spmd.clone.sunk | while | flops 707791424 | bytes 35652600 | solution.py:52
  44.1 4.4 copy.24
  49.2 6.6 %convolution_add_fusion.5 = f32[32,32768]{1,0:T(8,128)} fusion(f32[32,32768]{1,0:T(8,128)} %bitcast.49, f32[32,32768]{1,0:T(8,128)} %get-tuple-element.506, pred[]{:T(512)S(6)} %compare.6, s32[32]{0:T(128)S(1)} %dynamic_slice.60, pred[32]{0:T(512)(128)(4,1)S(1)} %add_compare_fusion.4), kind=kOutput, calls=%fused_computation.4.clone.1 | convolution fusion | flops 404752384 | bytes 12583073 | tf_op jit(solution)/shard_map/while/body/eval_jaxpr/dot_general | solution.py:43
  59.0 4.4 copy.24
  64.1 7.8 %convolution_add_fusion.5 = f32[32,32768]{1,0:T(8,128)} fusion(f32[32,32768]{1,0:T(8,128)} %bitcast.49, f32[32,32768]{1,0:T(8,128)} %get-tuple-element.506, pred[]{:T(512)S(6)} %compare.6, s32[32]{0:T(128)S(1)} %dynamic_slice.60, pred[32]{0:T(512)(128)(4,1)S(1)} %add_compare_fusion.4), kind=kOutput, calls=%fused_computation.4.clone.1 | convolution fusion | flops 404752384 | bytes 12583073 | tf_op jit(solution)/shard_map/while/body/eval_jaxpr/dot_general | solution.py:43
  75.1 4.4 copy.24
  80.2 7.8 %convolution_add_fusion.5 = f32[32,32768]{1,0:T(8,128)} fusion(f32[32,32768]{1,0:T(8,128)} %bitcast.49, f32[32,32768]{1,0:T(8,128)} %get-tuple-element.506, pred[]{:T(512)S(6)} %compare.6, s32[32]{0:T(128)S(1)} %dynamic_slice.60, pred[32]{0:T(512)(128)(4,1)S(1)} %add_compare_fusion.4), kind=kOutput, calls=%fused_computation.4.clone.1 | convolution fusion | flops 404752384 | bytes 12583073 | tf_op jit(solution)/shard_map/while/body/eval_jaxpr/dot_general | solution.py:43
  91.3 4.4 copy.24
  96.4 7.8 %convolution_add_fusion.5 = f32[32,32768]{1,0:T(8,128)} fusion(f32[32,32768]{1,0:T(8,128)} %bitcast.49, f32[32,32768]{1,0:T(8,128)} %get-tuple-element.506, pred[]{:T(512)S(6)} %compare.6, s32[32]{0:T(128)S(1)} %dynamic_slice.60, pred[32]{0:T(512)(128)(4,1)S(1)} %add_compare_fusion.4), kind=kOutput, calls=%fused_computation.4.clone.1 | convolution fusion | flops 404752384 | bytes 12583073 | tf_op jit(solution)/shard_map/while/body/eval_jaxpr/dot_general | solution.py:43
  107.5 4.4 copy.24
  112.6 7.8 %convolution_add_fusion.5 = f32[32,32768]{1,0:T(8,128)} fusion(f32[32,32768]{1,0:T(8,128)} %bitcast.49, f32[32,32768]{1,0:T(8,128)} %get-tuple-element.506, pred[]{:T(512)S(6)} %compare.6, s32[32]{0:T(128)S(1)} %dynamic_slice.60, pred[32]{0:T(512)(128)(4,1)S(1)} %add_compare_fusion.4), kind=kOutput, calls=%fused_computation.4.clone.1 | convolution fusion | flops 404752384 | bytes 12583073 | tf_op jit(solution)/shard_map/while/body/eval_jaxpr/dot_general | solution.py:43
  123.7 4.4 copy.24
  128.8 7.8 %convolution_add_fusion.5 = f32[32,32768]{1,0:T(8,128)} fusion(f32[32,32768]{1,0:T(8,128)} %bitcast.49, f32[32,32768]{1,0:T(8,128)} %get-tuple-element.506, pred[]{:T(512)S(6)} %compare.6, s32[32]{0:T(128)S(1)} %dynamic_slice.60, pred[32]{0:T(512)(128)(4,1)S(1)} %add_compare_fusion.4), kind=kOutput, calls=%fused_computation.4.clone.1 | convolution fusion | flops 404752384 | bytes 12583073 | tf_op jit(solution)/shard_map/while/body/eval_jaxpr/dot_general | solution.py:43
  139.9 4.4 copy.24
  145.0 7.8 %convolution_add_fusion.5 = f32[32,32768]{1,0:T(8,128)} fusion(f32[32,32768]{1,0:T(8,128)} %bitcast.49, f32[32,32768]{1,0:T(8,128)} %get-tuple-element.506, pred[]{:T(512)S(6)} %compare.6, s32[32]{0:T(128)S(1)} %dynamic_slice.60, pred[32]{0:T(512)(128)(4,1)S(1)} %add_compare_fusion.4), kind=kOutput, calls=%fused_computation.4.clone.1 | convolution fusion | flops 404752384 | bytes 12583073 | tf_op jit(solution)/shard_map/while/body/eval_jaxpr/dot_general | solution.py:43
  156.1 4.4 copy.24
  161.2 7.8 %convolution_add_fusion.5 = f32[32,32768]{1,0:T(8,128)} fusion(f32[32,32768]{1,0:T(8,128)} %bitcast.49, f32[32,32768]{1,0:T(8,128)} %get-tuple-element.506, pred[]{:T(512)S(6)} %compare.6, s32[32]{0:T(128)S(1)} %dynamic_slice.60, pred[32]{0:T(512)(128)(4,1)S(1)} %add_compare_fusion.4), kind=kOutput, calls=%fused_computation.4.clone.1 | convolution fusion | flops 404752384 | bytes 12583073 | tf_op jit(solution)/shard_map/while/body/eval_jaxpr/dot_general | solution.py:43
  172.3 4.4 copy.24
  177.4 7.8 %convolution_add_fusion.5 = f32[32,32768]{1,0:T(8,128)} fusion(f32[32,32768]{1,0:T(8,128)} %bitcast.49, f32[32,32768]{1,0:T(8,128)} %get-tuple-element.506, pred[]{:T(512)S(6)} %compare.6, s32[32]{0:T(128)S(1)} %dynamic_slice.60, pred[32]{0:T(512)(128)(4,1)S(1)} %add_compare_fusion.4), kind=kOutput, calls=%fused_computation.4.clone.1 | convolution fusion | flops 404752384 | bytes 12583073 | tf_op jit(solution)/shard_map/while/body/eval_jaxpr/dot_general | solution.py:43
  188.4 4.4 copy.24
  193.5 7.8 %convolution_add_fusion.5 = f32[32,32768]{1,0:T(8,128)} fusion(f32[32,32768]{1,0:T(8,128)} %bitcast.49, f32[32,32768]{1,0:T(8,128)} %get-tuple-element.506, pred[]{:T(512)S(6)} %compare.6, s32[32]{0:T(128)S(1)} %dynamic_slice.60, pred[32]{0:T(512)(128)(4,1)S(1)} %add_compare_fusion.4), kind=kOutput, calls=%fused_computation.4.clone.1 | convolution fusion | flops 404752384 | bytes 12583073 | tf_op jit(solution)/shard_map/while/body/eval_jaxpr/dot_general | solution.py:43
  204.6 4.4 copy.24
  209.7 7.8 %convolution_add_fusion.5 = f32[32,32768]{1,0:T(8,128)} fusion(f32[32,32768]{1,0:T(8,128)} %bitcast.49, f32[32,32768]{1,0:T(8,128)} %get-tuple-element.506, pred[]{:T(512)S(6)} %compare.6, s32[32]{0:T(128)S(1)} %dynamic_slice.60, pred[32]{0:T(512)(128)(4,1)S(1)} %add_compare_fusion.4), kind=kOutput, calls=%fused_computation.4.clone.1 | convolution fusion | flops 404752384 | bytes 12583073 | tf_op jit(solution)/shard_map/while/body/eval_jaxpr/dot_general | solution.py:43
  220.8 4.4 copy.24
  225.9 7.8 %convolution_add_fusion.5 = f32[32,32768]{1,0:T(8,128)} fusion(f32[32,32768]{1,0:T(8,128)} %bitcast.49, f32[32,32768]{1,0:T(8,128)} %get-tuple-element.506, pred[]{:T(512)S(6)} %compare.6, s32[32]{0:T(128)S(1)} %dynamic_slice.60, pred[32]{0:T(512)(128)(4,1)S(1)} %add_compare_fusion.4), kind=kOutput, calls=%fused_computation.4.clone.1 | convolution fusion | flops 404752384 | bytes 12583073 | tf_op jit(solution)/shard_map/while/body/eval_jaxpr/dot_general | solution.py:43
  233.7 4.9 reshape_reshape.11
  238.7 50.1 %reduce-scatter.3.cloned.1.call-done = f32[512,256]{1,0:T(8,128)} async-done(((f32[4096,256]{1,0:T(8,128)}), f32[512,256]{1,0:T(8,128)}) %reduce-scatter.3.cloned.1.call-update) | async-done | bytes 524304 | tf_op jit(solution)/shard_map/reduce_scatter | solution.py:75
  292.0 16.7 %copy.12 = bf16[1,1,384,128,128]{3,4,2,1,0:T(8,128)(2,1)} copy(bf16[1,1,384,128,128]{4,3,2,1,0:T(8,128)(2,1)} %bitcast.58) | data formatting | bytes 25165824 | tf_op args[4]
  310.0 9.4 %all-gather.5.cloned.1.call-done = bf16[4096,256]{1,0:T(8,128)(2,1)} async-done(((bf16[512,256]{1,0:T(8,128)(2,1)}), bf16[4096,256]{1,0:T(8,128)(2,1)}) %all-gather.5.cloned.1.call-update) | async-done | bytes 2097168 | tf_op jit(solution)/shard_map/all_gather | solution.py:85
  319.4 4.2 reshape_reshape.12
  323.6 163.7 %while.29 = (s32[]{:T(128)}, f32[16,32768]{1,0:T(8,128)S(1)}, s32[384]{0:T(512)S(1)}, s32[]{:T(128)}, bf16[384,128,128]{1,2,0:T(8,128)(2,1)}, /*index=5*/s32[384...) while((s32[]{:T(128)}, f32[16,32768]{1,0:T(8,128)S(1)}, ...), condition=%wide.region_7.8_spmd.clone, body=%wide.region_6.7_spmd.clone.sunk | while | flops 538970176 | bytes 32506872 | solution.py:52
  328.4 4.4 copy.26
  333.5 3.6 convolution_add_fusion.6
  342.1 4.4 copy.26
  347.2 3.6 convolution_add_fusion.6
  355.7 4.4 copy.26
  360.8 3.6 convolution_add_fusion.6
  369.4 4.4 copy.26
  383.0 4.4 copy.26
  396.7 4.4 copy.26
  410.3 4.4 copy.26
  424.0 4.4 copy.26
  437.6 4.4 copy.26
  451.3 4.4 copy.26
  464.9 4.4 copy.26
  478.5 4.4 copy.26
  488.8 40.2 %psum.15 = f32[256]{0:T(256)S(1)} all-reduce(f32[256]{0:T(256)S(1)} %get-tuple-element.405), channel_id=1, replica_groups=mesh['row'=4,'col'=8] {'row','col'}, use_global_device_ids=true, to_apply=%region_5.6 | all-reduce | flops 256 | bytes 2048 | tf_op jit(solution)/shard_map/psum | solution.py:94
  (187 shorter events, 159.0 us)
Async XLA Ops:
  7.2 281.6 %copy-start = (bf16[256,256]{1,0:T(8,128)(2,1)S(1)}, bf16[256,256]{1,0:T(8,128)(2,1)}, u32[]{:S(2)}) copy-start(bf16[256,256]{1,0:T(8,128)(2,1)} %param.13) | copy-start | bytes 393220
  7.2 32.0 %all-gather.3.cloned.1.call-start = ((), (), s32[]{:S(2)}) async-start(), calls=%async_computation.2 | async-start | bytes 1310720 | tf_op jit(solution)/shard_map/all_gather | solution.py:69
  7.9 280.9 %reduce-scatter.3.cloned.1.call-start = ((), (), s32[]{:S(2)}) async-start(), calls=%async_computation.3 | async-start | bytes 4718592 | tf_op jit(solution)/shard_map/reduce_scatter | solution.py:75
  238.6 50.2 %copy-start.3 = (bf16[512,256]{1,0:T(8,128)(2,1)S(1)}, bf16[512,256]{1,0:T(8,128)(2,1)}, u32[]{:S(2)}) copy-start(bf16[512,256]{1,0:T(8,128)(2,1)} %param.15) | copy-start | bytes 786436
  238.6 50.2 %copy-start.4 = (f32[256]{0:T(256)S(1)}, f32[256]{0:T(256)}, u32[]{:S(2)}) copy-start(f32[256]{0:T(256)} %param.14) | copy-start | bytes 3076
  238.6 80.7 %all-gather.5.cloned.1.call-start = ((), (), s32[]{:S(2)}) async-start(), calls=%async_computation.5 | async-start | bytes 2359296 | tf_op jit(solution)/shard_map/all_gather | solution.py:85
  292.0 16.8 %copy-start.2 = (f32[512,256]{1,0:T(8,128)S(1)}, f32[512,256]{1,0:T(8,128)}, u32[]{:S(2)}) copy-start(f32[512,256]{1,0:T(8,128)} %reduce-scatter.3.cloned.1.call-done) | copy-start | bytes 1572868
  292.0 237.6 %all-reduce.2.cloned.1.call-start = ((), (), s32[]{:S(2)}) async-start(), calls=%async_computation.4 | async-start | bytes 524288 | tf_op jit(solution)/shard_map/psum | solution.py:94
  309.8 221.5 %reduce-scatter.5.cloned.1.call-start = ((), (), s32[]{:S(2)}) async-start(), calls=%async_computation.6 | async-start | bytes 1310720 | tf_op jit(solution)/shard_map/reduce_scatter | solution.py:91
  487.3 43.9 %copy-start.1 = (bf16[256,256]{1,0:T(8,128)(2,1)S(1)}, bf16[256,256]{1,0:T(8,128)(2,1)}, u32[]{:S(2)}) copy-start(bf16[256,256]{1,0:T(8,128)(2,1)} %param.13) | copy-start | bytes 393220
Sparse Core Ops, SparseCore 0:
  9.9 29.3 all-gather.2
  238.8 49.9 reduce-scatter.2
  292.1 27.2 all-gather.4
  325.3 124.5 all-reduce.1
  488.9 27.2 reduce-scatter.4
where the time goes:
time: 540 us; the launch traced here: 538 us
  matrix products  224 us (41%)
  local copies, waits for them, and re-layouts  149 us (28%)
  waiting for transfers between devices  90.1 us (17%)
  blocking collectives  40.2 us (7%)
  other arithmetic  19.3 us (4%)
  between operations  13.8 us (3%)
    dot_general x24, matrix products, one_group(): jnp.dot(placer.T, contrib.reshape(group, block * width), precision=lax.Pr...  136 us
    while x48, local copies, waits for them, and re-layouts  117 us
    reduce_scatter x1, waiting for transfers between devices, per_device(): summed = lax.psum_scatter(term, 'col', scatter_dimension=0, tiled=True)  50.1 us
    psum x1, blocking collectives, per_device(): lax.psum((local_weight, local_bias), ('row', 'col'))  40.2 us
    dot_general x24, matrix products, one_group(): fetched = jnp.dot(picker, flat_source, preferred_element_type=jnp.float32)  37.1 us
    all_gather x1, waiting for transfers between devices, per_device(): panel = lax.all_gather(features, 'row', axis=0, tiled=True)  29.8 us
    dot_general x12, matrix products, one_group(): jnp.einsum('tji,tjf->tif', tile_group, fetched, preferred_element_type=jn...  23.2 us
    dot_general x12, matrix products, one_group(): jnp.einsum('tij,tjf->tif', tile_group, fetched, preferred_element_type=jn...  23.2 us
  transfers between devices with their start and end apart: 5, of which 3 were waited for; matrix products, arithmetic and copies ran while one was open for 35% of the time, Pallas kernels for 0%

commit v1 on v0

v1 whole, which is shorter than its diff:
```python
import math

import jax
import jax.numpy as jnp
from jax import lax
from jax.experimental import pallas as pl
from jax.experimental.pallas import tpu as pltpu
from jax.sharding import PartitionSpec as P


def densify_kernel(count_ref, rows_ref, cols_ref, tiles_ref, cell_ref, present, zero, sem):
    slots, block, _ = tiles_ref.shape
    blocks_down = cell_ref.shape[0] // block
    blocks_across = cell_ref.shape[1] // block
    blocks = blocks_down * blocks_across

    def place(row, col):
        return cell_ref.at[
            pl.ds(pl.multiple_of(row * block, block), block),
            pl.ds(pl.multiple_of(col * block, block), block),
        ]

    def clear(index, carry):
        present[index] = 0
        return carry

    lax.fori_loop(0, blocks, clear, 0, unroll=8)
    zero[...] = jnp.zeros_like(zero)
    count = count_ref[0]

    def put_tile(slot, carry):
        row = rows_ref[slot]
        col = cols_ref[slot]
        present[row * blocks_across + col] = 1
        pltpu.make_async_copy(tiles_ref.at[slot], place(row, col), sem).start()
        return carry

    lax.fori_loop(0, count, put_tile, 0)

    def put_zero(index, carry):
        @pl.when(present[index] == 0)
        def _():
            row = index // blocks_across
            col = index % blocks_across
            pltpu.make_async_copy(zero, place(row, col), sem).start()

        return carry

    lax.fori_loop(0, blocks, put_zero, 0)

    def wait_one(index, carry):
        pltpu.make_async_copy(zero, place(0, 0), sem).wait()
        return carry

    lax.fori_loop(0, blocks, wait_one, 0)


def densify(tiles, rows, cols, count, blocks_down, blocks_across):
    block = tiles.shape[-1]
    shape = (blocks_down * block, blocks_across * block)
    size = shape[0] * shape[1] * 2
    return pl.pallas_call(
        densify_kernel,
        out_shape=jax.ShapeDtypeStruct(shape, tiles.dtype),
        in_specs=[
            pl.BlockSpec(memory_space=pltpu.SMEM),
            pl.BlockSpec(memory_space=pltpu.SMEM),
            pl.BlockSpec(memory_space=pltpu.SMEM),
            pl.BlockSpec(memory_space=pl.ANY),
        ],
        out_specs=pl.BlockSpec(memory_space=pl.ANY),
        scratch_shapes=[
            pltpu.SMEM((blocks_down * blocks_across,), jnp.int32),
            pltpu.VMEM((block, block), tiles.dtype),
            pltpu.SemaphoreType.DMA,
        ],
        cost_estimate=pl.CostEstimate(flops=0, bytes_accessed=2 * size, transcendentals=0),
        name="densify",
    )(count, rows, cols, tiles)


def swap(value, axis, mask):
    count = lax.axis_size(axis)
    return lax.ppermute(value, axis, [(i, i ^ mask) for i in range(count)])


def per_device(features, weight, bias, cotangent, tiles, tile_rows, tile_cols, tile_counts):
    tile_set = tiles[0, 0]
    block = tile_set.shape[-1]
    nodes, width = features.shape
    row_count = lax.axis_size("row")
    col_count = lax.axis_size("col")
    half = col_count // 2
    row_pos = lax.axis_index("row")
    col_pos = lax.axis_index("col")
    per = nodes // block
    factor = 1.0 / math.sqrt(nodes * row_count * col_count)
    f32 = jnp.float32
    bf16 = jnp.bfloat16

    down = (tile_rows[0, 0] // per) ^ col_pos
    down = (down & 1) * half + (down >> 1)
    rows = down * per + tile_rows[0, 0] % per
    across = (tile_cols[0, 0] // per) ^ row_pos
    cols = across * per + tile_cols[0, 0] % per

    panels = [features] + [swap(features, "row", k) for k in range(1, row_count)]
    cell = densify(
        tile_set, rows, cols, tile_counts[0], per * col_count, per * row_count
    )
    own_cell = cell[: half * nodes]
    mate_cell = cell[half * nodes :]
    source = jnp.concatenate(panels, axis=0)

    for_mate = jnp.dot(mate_cell, source, preferred_element_type=f32).astype(bf16)
    from_mate = swap(for_mate, "col", 1)
    own_part = jnp.dot(own_cell, source, preferred_element_type=f32)
    own_part = own_part + from_mate.astype(f32)
    total = own_part[:nodes]
    arrived = [
        swap(own_part[k * nodes : (k + 1) * nodes].astype(bf16), "col", 2 * k)
        for k in range(1, half)
    ]
    for part in arrived:
        total = total + part.astype(f32)

    aggregated = total.astype(bf16)
    preact = jnp.dot(aggregated, weight, preferred_element_type=f32) + bias
    sigma = jax.nn.sigmoid(preact)
    hidden = (preact * sigma).astype(bf16)
    slope = sigma * (1.0 + preact * (1.0 - sigma))
    grad_pre = (cotangent.astype(f32) * slope).astype(bf16)
    grad_agg = lax.dot_general(
        weight, grad_pre, (((1,), (1,)), ((), ())), preferred_element_type=f32
    ).astype(bf16)

    own_grads = [grad_agg] + [swap(grad_agg, "col", 2 * k) for k in range(1, half)]
    mate_grads = [swap(part, "col", 1) for part in own_grads]

    local_weight = jnp.einsum("nf,ng->fg", aggregated, grad_pre, preferred_element_type=f32)
    local_bias = jnp.sum(grad_pre.astype(f32), axis=0, keepdims=True)
    local = jnp.concatenate(
        [local_weight, jnp.broadcast_to(local_bias, (8, width))], axis=0
    )
    summed = lax.psum(local, ("row", "col")) * factor
    grad_weight = summed[:width]
    grad_bias = summed[width]

    back = jnp.dot(
        jnp.concatenate(own_grads, axis=1), own_cell, preferred_element_type=f32
    )
    back = back + jnp.dot(
        jnp.concatenate(mate_grads, axis=1), mate_cell, preferred_element_type=f32
    )
    result = back[:, :nodes]
    pieces = [
        swap(back[:, k * nodes : (k + 1) * nodes].astype(bf16), "row", k)
        for k in range(1, row_count)
    ]
    for piece in pieces:
        result = result + piece.astype(f32)
    grad_features = result.astype(bf16).T
    return (hidden, grad_weight, grad_bias, grad_features)


def solution(mesh):
    in_specs = (
        P(("col", "row"), None),
        P(),
        P(),
        P(("row", "col"), None),
        P("row", "col", None, None, None),
        P("row", "col", None),
        P("row", "col", None),
        P("row", "col"),
    )
    out_specs = (P(("row", "col"), None), P(), P(), P(("col", "row"), None))
    return jax.shard_map(
        per_device, mesh=mesh, in_specs=in_specs, out_specs=out_specs, check_vma=False
    )
```

time: 540 us -> 584 us (1.081)
  starting transfers between devices: 0.38 us -> 303 us
  matrix products: 224 us -> 22.9 us
  local copies, waits for them, and re-layouts: 149 us -> 3.29 us
  Pallas kernels: 0 us -> 97.8 us
  waiting for transfers between devices: 90.1 us -> 136 us
  blocking collectives: 40.2 us -> 0 us
  other arithmetic: 19.3 us -> 5.03 us
    ppermute x0 -> x17, starting transfers between devices: none -> 303 us  [swap(): return lax.ppermute(value, axis, [(i, i ^ mask) for i in range(count)])]
    dot_general x75 -> x7, matrix products: 224 us -> 22.9 us  [the longest x1 7.09 us: per_device(): jnp.dot(jnp.concatenate(mate_grads, axis=1), mate_cell, preferred_element...]
    while x48 -> x0, local copies, waits for them, and re-layouts: 117 us -> none
    pallas_call x0 -> x1, Pallas kernels: none -> 97.8 us  [densify(): pl.pallas_call(densify_kernel, out_shape=jax.ShapeDtypeStruct(shape, tile...]
    psum x1, waiting for transfers between devices: 0.01 us -> 91 us  [per_device(): summed = lax.psum(local, ('row', 'col')) * factor]
    reduce_scatter x2 -> x0, waiting for transfers between devices: 50.1 us -> none  [the longest x1 50.1 us: per_device(): summed = lax.psum_scatter(term, 'col', scatter_dimension=0, tiled=True)]
    ppermute x0 -> x17, waiting for transfers between devices: none -> 45.2 us  [swap(): return lax.ppermute(value, axis, [(i, i ^ mask) for i in range(count)])]
    psum x1 -> x0, blocking collectives: 40.2 us -> none  [per_device(): lax.psum((local_weight, local_bias), ('row', 'col'))]
  transfers between devices with their start and end apart: 5 -> 18, of which waited for: 3 -> 6; matrix products, arithmetic and copies ran while one was open for 35% -> 3% of each run, Pallas kernels for 0% -> 17%
where the time goes in v1:
time: 584 us; the launch traced here: 583 us
  starting transfers between devices  303 us (52%)
  waiting for transfers between devices  136 us (23%)
  Pallas kernels  97.8 us (17%)
  matrix products  22.9 us (4%)
  between operations  14.9 us (3%)
    ppermute x17, starting transfers between devices, swap(): return lax.ppermute(value, axis, [(i, i ^ mask) for i in range(count)])  303 us
    pallas_call x1, Pallas kernels, densify(): pl.pallas_call(densify_kernel, out_shape=jax.ShapeDtypeStruct(shape, tile...  97.8 us
    psum x1, waiting for transfers between devices, per_device(): summed = lax.psum(local, ('row', 'col')) * factor  91 us
    ppermute x17, waiting for transfers between devices, swap(): return lax.ppermute(value, axis, [(i, i ^ mask) for i in range(count)])  45.2 us
  transfers between devices with their start and end apart: 18, of which 6 were waited for; matrix products, arithmetic and copies ran while one was open for 3% of the time, Pallas kernels for 17%

profile of v1, /device:TPU:0, one launch (start us, length us, event | category | flops | bytes accessed | tf_op | source)
XLA Modules:
  0.0 583.3 jit_solution(16263199764363151745)
XLA Ops:
  7.2 0.0 copy-start
  7.2 0.0 all-reduce.2.cloned.1.call-start
  7.2 3.0 collective-permute-start.1
  10.3 1.5 collective-permute-start
  11.8 0.1 collective-permute-start.2
  11.8 0.7 reduce
  12.5 0.7 reduce.1
  13.2 0.6 fusion.40
  13.8 1.0 constant_dynamic-update-slice_fusion.3
  15.4 97.8 %densify.1 = bf16[4096,2048]{1,0:T(8,128)(2,1)} custom-call(s32[1]{0:T(128)} %bitcast.15.count_ref, s32[384]{0:T(512)} %get-tuple-element.21.rows_ref, s32[384]{0:T(512)} %get-tuple-element.22.cols_ref, bf16[384,128,128]{2,1,0:T(8,128)(2,1)} %bitcast.16), custom_call_target="tpu_custom_call" | custom-call | bytes 33554432 | tf_op jit(solution)/shard_map/densify/pallas_call | solution.py:62
  113.2 0.0 collective-permute-done
  113.2 0.0 collective-permute-done.1
  113.3 5.9 %fusion.14 = bf16[2048,256]{1,0:T(8,128)(2,1)S(1)} fusion(bf16[2048,256]{1,0:T(8,128)(2,1)S(1)} %constant_dynamic-update-slice_fusion, bf16[4096,2048]{1,0:T(8,128)(2,1)} %densify.1), kind=kOutput, calls=%fused_computation.10 | convolution fusion | flops 2148007936 | bytes 10485760 | tf_op jit(solution)/shard_map/dot_general | solution.py:115
  119.2 0.1 collective-permute-start.3
  119.3 2.6 collective-permute-done.3
  121.9 2.5 fusion.52
  124.5 0.0 copy-start.2
  124.5 0.0 copy-start.3
  124.5 0.1 fusion.51
  124.6 96.0 %collective-permute-start.4 = (bf16[512,256]{1,0:T(8,128)(2,1)S(1)}, bf16[512,256]{1,0:T(8,128)(2,1)S(1)}, u32[]{:S(2)}, u32[]{:S(2)}) collective-permute-start(bf16[512,256]{1,0:T(8,128)(2,1)S(1)} %get-tuple-element.13), channel_id=1, source_target_pairs={{0,2},{1,3},{2,0},{3,1},{4,6},{5,7},{6,4},{7,5},{8,10},{9,11},{10,... | collective-permute-start | bytes 786440 | tf_op jit(solution)/shard_map/ppermute | solution.py:84
  220.6 98.8 %collective-permute-start.6 = (bf16[512,256]{1,0:T(8,128)(2,1)S(1)}, bf16[512,256]{1,0:T(8,128)(2,1)S(1)}, u32[]{:S(2)}, u32[]{:S(2)}) collective-permute-start(bf16[512,256]{1,0:T(8,128)(2,1)S(1)} %get-tuple-element.14), channel_id=1, source_target_pairs={{0,6},{1,7},{2,4},{3,5},{4,2},{5,3},{6,0},{7,1},{8,14},{9,15},{10,... | collective-permute-start | bytes 786440 | tf_op jit(solution)/shard_map/ppermute | solution.py:84
  319.3 0.5 collective-permute-start.5
  319.8 12.2 %collective-permute-done.6 = bf16[512,256]{1,0:T(8,128)(2,1)S(1)} collective-permute-done((bf16[512,256]{1,0:T(8,128)(2,1)S(1)}, bf16[512,256]{1,0:T(8,128)(2,1)S(1)}, u32[]{:S(2)}, u32[]{:S(2)}) %collective-permute-start.6) | collective-permute-done | bytes 262176 | tf_op jit(solution)/shard_map/ppermute | solution.py:84
  332.1 10.9 %collective-permute-done.5 = bf16[512,256]{1,0:T(8,128)(2,1)S(1)} collective-permute-done((bf16[512,256]{1,0:T(8,128)(2,1)S(1)}, bf16[512,256]{1,0:T(8,128)(2,1)S(1)}, u32[]{:S(2)}, u32[]{:S(2)}) %collective-permute-start.5) | collective-permute-done | bytes 262176 | tf_op jit(solution)/shard_map/ppermute | solution.py:84
  343.0 0.2 fusion.37
  343.2 1.1 convert_reduce_fusion
  344.3 0.3 fusion.17
  344.6 0.1 collective-permute-start.10
  344.6 2.7 collective-permute-start.9
  347.4 1.7 collective-permute-start.7
  349.1 0.3 fusion.54
  349.4 0.7 pad_maximum_fusion
  350.1 0.0 all-reduce.2.cloned.1.call-update
  350.1 5.6 collective-permute-done.9
  355.8 13.7 %collective-permute-done.8 = bf16[256,512]{0,1:T(8,128)(2,1)S(1)} collective-permute-done((bf16[256,512]{0,1:T(8,128)(2,1)S(1)}, bf16[256,512]{0,1:T(8,128)(2,1)S(1)}, u32[]{:S(2)}, u32[]{:S(2)}) %collective-permute-start.8) | collective-permute-done | bytes 262176 | tf_op jit(solution)/shard_map/ppermute | solution.py:84
  369.5 0.5 collective-permute-start.11
  370.0 5.7 fusion.4
  375.8 7.1 %fusion.53 = (bf16[256,2048]{1,0:T(8,128)(2,1)S(1)}, f32[256,2048]{1,0:T(8,128)}) fusion(f32[256,2048]{1,0:T(8,128)S(1)} %fusion.4, bf16[4096,2048]{1,0:T(8,128)(2,1)} %densify.1, bf16[256,512]{0,1:T(8,128)(2,1)S(1)} %collective-permute-done.13, bf16[256,512]{0,1:T(8,128)(2,1)S(1)} %collective-permute-done.12, ...), kind=kOutput, calls=%fused_computation.73 | convolution fusion | flops 2152726528 | bytes 14680064 | tf_op jit(solution)/shard_map/dot_general | solution.py:152
  382.9 0.1 fusion.50
  382.9 96.7 %collective-permute-start.14 = (bf16[256,512]{1,0:T(8,128)(2,1)S(1)}, bf16[256,512]{1,0:T(8,128)(2,1)S(1)}, u32[]{:S(2)}, u32[]{:S(2)}) collective-permute-start(bf16[256,512]{1,0:T(8,128)(2,1)S(1)} %get-tuple-element.10), channel_id=1, source_target_pairs={{0,8},{8,0},{16,24},{24,16},{1,9},{9,1},{17,25},{25,17},{2,10},{10... | collective-permute-start | bytes 786440 | tf_op jit(solution)/shard_map/ppermute | solution.py:84
  479.6 0.2 collective-permute-start.16
  479.8 1.3 collective-permute-start.15
  481.2 91.0 %all-reduce.2.cloned.1.call-done = f32[264,256]{1,0:T(8,128)} async-done(((f32[264,256]{1,0:T(8,128)}), f32[264,256]{1,0:T(8,128)}) %all-reduce.2.cloned.1.call-update) | async-done | bytes 270352 | tf_op jit(solution)/shard_map/psum | solution.py:145
  572.2 1.0 broadcast_multiply_fusion
  573.2 0.6 slice.61
  573.7 0.7 slice.60
  574.5 1.2 fusion.38
  575.6 0.8 copy.12
  (22 shorter events, 0.1 us)
Async XLA Ops:
  7.2 336.0 %copy-start = (bf16[256,256]{1,0:T(8,128)(2,1)S(1)}, bf16[256,256]{1,0:T(8,128)(2,1)}, u32[]{:S(2)}) copy-start(bf16[256,256]{1,0:T(8,128)(2,1)} %param.9) | copy-start | bytes 393220
  7.2 565.0 %all-reduce.2.cloned.1.call-start = ((), (), s32[]{:S(2)}) async-start(), calls=%async_computation | async-start | bytes 540672 | tf_op jit(solution)/shard_map/psum | solution.py:145
  7.2 106.0 %collective-permute-start.1 = (bf16[512,256]{1,0:T(8,128)(2,1)}, bf16[512,256]{1,0:T(8,128)(2,1)S(1)}, u32[]{:S(2)}, u32[]{:S(2)}) collective-permute-start(bf16[512,256]{1,0:T(8,128)(2,1)} %param.8), channel_id=1, source_target_pairs={{0,16},{8,24},{16,0},{24,8},{1,17},{9,25},{17,1},{25,9},{2,18},{10... | collective-permute-start | bytes 786440 | tf_op jit(solution)/shard_map/ppermute | solution.py:84
  10.3 102.9 %collective-permute-start = (bf16[512,256]{1,0:T(8,128)(2,1)}, bf16[512,256]{1,0:T(8,128)(2,1)S(1)}, u32[]{:S(2)}, u32[]{:S(2)}) collective-permute-start(bf16[512,256]{1,0:T(8,128)(2,1)} %param.8), channel_id=1, source_target_pairs={{0,8},{8,0},{16,24},{24,16},{1,9},{9,1},{17,25},{25,17},{2,10},{10... | collective-permute-start | bytes 786440 | tf_op jit(solution)/shard_map/ppermute | solution.py:84
  11.8 101.5 %collective-permute-start.2 = (bf16[512,256]{1,0:T(8,128)(2,1)}, bf16[512,256]{1,0:T(8,128)(2,1)S(1)}, u32[]{:S(2)}, u32[]{:S(2)}) collective-permute-start(bf16[512,256]{1,0:T(8,128)(2,1)} %param.8), channel_id=1, source_target_pairs={{0,24},{8,16},{16,8},{24,0},{1,25},{9,17},{17,9},{25,1},{2,26},{10... | collective-permute-start | bytes 786440 | tf_op jit(solution)/shard_map/ppermute | solution.py:84
  113.3 8.6 %copy-start.1 = (bf16[4096,2048]{1,0:T(8,128)(2,1)S(1)}, bf16[4096,2048]{1,0:T(8,128)(2,1)}, u32[]{:S(2)}) copy-start(bf16[4096,2048]{1,0:T(8,128)(2,1)} %densify.1) | copy-start | bytes 50331652
  119.2 2.7 collective-permute-start.3
  124.5 218.7 %copy-start.2 = (bf16[512,256]{1,0:T(8,128)(2,1)S(1)}, bf16[512,256]{1,0:T(8,128)(2,1)}, u32[]{:S(2)}) copy-start(bf16[512,256]{1,0:T(8,128)(2,1)} %param.11) | copy-start | bytes 786436
  124.5 218.7 %copy-start.3 = (f32[256]{0:T(256)S(1)}, f32[256]{0:T(256)}, u32[]{:S(2)}) copy-start(f32[256]{0:T(256)} %param.10) | copy-start | bytes 3076
  124.6 195.2 %collective-permute-start.4 = (bf16[512,256]{1,0:T(8,128)(2,1)S(1)}, bf16[512,256]{1,0:T(8,128)(2,1)S(1)}, u32[]{:S(2)}, u32[]{:S(2)}) collective-permute-start(bf16[512,256]{1,0:T(8,128)(2,1)S(1)} %get-tuple-element.13), channel_id=1, source_target_pairs={{0,2},{1,3},{2,0},{3,1},{4,6},{5,7},{6,4},{7,5},{8,10},{9,11},{10,... | collective-permute-start | bytes 786440 | tf_op jit(solution)/shard_map/ppermute | solution.py:84
  220.6 111.5 %collective-permute-start.6 = (bf16[512,256]{1,0:T(8,128)(2,1)S(1)}, bf16[512,256]{1,0:T(8,128)(2,1)S(1)}, u32[]{:S(2)}, u32[]{:S(2)}) collective-permute-start(bf16[512,256]{1,0:T(8,128)(2,1)S(1)} %get-tuple-element.14), channel_id=1, source_target_pairs={{0,6},{1,7},{2,4},{3,5},{4,2},{5,3},{6,0},{7,1},{8,14},{9,15},{10,... | collective-permute-start | bytes 786440 | tf_op jit(solution)/shard_map/ppermute | solution.py:84
  319.3 23.7 %collective-permute-start.5 = (bf16[512,256]{1,0:T(8,128)(2,1)S(1)}, bf16[512,256]{1,0:T(8,128)(2,1)S(1)}, u32[]{:S(2)}, u32[]{:S(2)}) collective-permute-start(bf16[512,256]{1,0:T(8,128)(2,1)S(1)} %get-tuple-element.15), channel_id=1, source_target_pairs={{0,4},{1,5},{2,6},{3,7},{4,0},{5,1},{6,2},{7,3},{8,12},{9,13},{10,... | collective-permute-start | bytes 786440 | tf_op jit(solution)/shard_map/ppermute | solution.py:84
  344.6 31.2 %collective-permute-start.10 = (bf16[256,512]{0,1:T(8,128)(2,1)S(1)}, bf16[256,512]{0,1:T(8,128)(2,1)S(1)}, u32[]{:S(2)}, u32[]{:S(2)}) collective-permute-start(bf16[256,512]{0,1:T(8,128)(2,1)S(1)} %fusion.17), channel_id=1, source_target_pairs={{0,1},{1,0},{2,3},{3,2},{4,5},{5,4},{6,7},{7,6},{8,9},{9,8},{10,11... | collective-permute-start | bytes 786440 | tf_op jit(solution)/shard_map/ppermute | solution.py:84
  344.6 11.1 %collective-permute-start.9 = (bf16[256,512]{0,1:T(8,128)(2,1)S(1)}, bf16[256,512]{0,1:T(8,128)(2,1)S(1)}, u32[]{:S(2)}, u32[]{:S(2)}) collective-permute-start(bf16[256,512]{0,1:T(8,128)(2,1)S(1)} %fusion.17), channel_id=1, source_target_pairs={{0,6},{1,7},{2,4},{3,5},{4,2},{5,3},{6,0},{7,1},{8,14},{9,15},{10,... | collective-permute-start | bytes 786440 | tf_op jit(solution)/shard_map/ppermute | solution.py:84
  347.4 22.1 %collective-permute-start.8 = (bf16[256,512]{0,1:T(8,128)(2,1)S(1)}, bf16[256,512]{0,1:T(8,128)(2,1)S(1)}, u32[]{:S(2)}, u32[]{:S(2)}) collective-permute-start(bf16[256,512]{0,1:T(8,128)(2,1)S(1)} %fusion.17), channel_id=1, source_target_pairs={{0,4},{1,5},{2,6},{3,7},{4,0},{5,1},{6,2},{7,3},{8,12},{9,13},{10,... | collective-permute-start | bytes 786440 | tf_op jit(solution)/shard_map/ppermute | solution.py:84
  347.4 22.1 %collective-permute-start.7 = (bf16[256,512]{0,1:T(8,128)(2,1)S(1)}, bf16[256,512]{0,1:T(8,128)(2,1)S(1)}, u32[]{:S(2)}, u32[]{:S(2)}) collective-permute-start(bf16[256,512]{0,1:T(8,128)(2,1)S(1)} %fusion.17), channel_id=1, source_target_pairs={{0,2},{1,3},{2,0},{3,1},{4,6},{5,7},{6,4},{7,5},{8,10},{9,11},{10,... | collective-permute-start | bytes 786440 | tf_op jit(solution)/shard_map/ppermute | solution.py:84
  355.8 20.0 %collective-permute-start.13 = (bf16[256,512]{0,1:T(8,128)(2,1)S(1)}, bf16[256,512]{0,1:T(8,128)(2,1)S(1)}, u32[]{:S(2)}, u32[]{:S(2)}) collective-permute-start(bf16[256,512]{0,1:T(8,128)(2,1)S(1)} %collective-permute-done.9), channel_id=1, source_target_pairs={{0,1},{1,0},{2,3},{3,2},{4,5},{5,4},{6,7},{7,6},{8,9},{9,8},{10,11... | collective-permute-start | bytes 786440 | tf_op jit(solution)/shard_map/ppermute | solution.py:84
  369.5 6.3 %collective-permute-start.12 = (bf16[256,512]{0,1:T(8,128)(2,1)S(1)}, bf16[256,512]{0,1:T(8,128)(2,1)S(1)}, u32[]{:S(2)}, u32[]{:S(2)}) collective-permute-start(bf16[256,512]{0,1:T(8,128)(2,1)S(1)} %collective-permute-done.8), channel_id=1, source_target_pairs={{0,1},{1,0},{2,3},{3,2},{4,5},{5,4},{6,7},{7,6},{8,9},{9,8},{10,11... | collective-permute-start | bytes 786440 | tf_op jit(solution)/shard_map/ppermute | solution.py:84
  369.5 6.3 %collective-permute-start.11 = (bf16[256,512]{0,1:T(8,128)(2,1)S(1)}, bf16[256,512]{0,1:T(8,128)(2,1)S(1)}, u32[]{:S(2)}, u32[]{:S(2)}) collective-permute-start(bf16[256,512]{0,1:T(8,128)(2,1)S(1)} %collective-permute-done.7), channel_id=1, source_target_pairs={{0,1},{1,0},{2,3},{3,2},{4,5},{5,4},{6,7},{7,6},{8,9},{9,8},{10,11... | collective-permute-start | bytes 786440 | tf_op jit(solution)/shard_map/ppermute | solution.py:84
  382.9 191.5 %collective-permute-start.14 = (bf16[256,512]{1,0:T(8,128)(2,1)S(1)}, bf16[256,512]{1,0:T(8,128)(2,1)S(1)}, u32[]{:S(2)}, u32[]{:S(2)}) collective-permute-start(bf16[256,512]{1,0:T(8,128)(2,1)S(1)} %get-tuple-element.10), channel_id=1, source_target_pairs={{0,8},{8,0},{16,24},{24,16},{1,9},{9,1},{17,25},{25,17},{2,10},{10... | collective-permute-start | bytes 786440 | tf_op jit(solution)/shard_map/ppermute | solution.py:84
  479.6 94.8 %collective-permute-start.16 = (bf16[256,512]{1,0:T(8,128)(2,1)S(1)}, bf16[256,512]{1,0:T(8,128)(2,1)S(1)}, u32[]{:S(2)}, u32[]{:S(2)}) collective-permute-start(bf16[256,512]{1,0:T(8,128)(2,1)S(1)} %get-tuple-element.11), channel_id=1, source_target_pairs={{0,24},{8,16},{16,8},{24,0},{1,25},{9,17},{17,9},{25,1},{2,26},{10... | collective-permute-start | bytes 786440 | tf_op jit(solution)/shard_map/ppermute | solution.py:84
  479.8 94.6 %collective-permute-start.15 = (bf16[256,512]{1,0:T(8,128)(2,1)S(1)}, bf16[256,512]{1,0:T(8,128)(2,1)S(1)}, u32[]{:S(2)}, u32[]{:S(2)}) collective-permute-start(bf16[256,512]{1,0:T(8,128)(2,1)S(1)} %get-tuple-element.12), channel_id=1, source_target_pairs={{0,16},{8,24},{16,0},{24,8},{1,17},{9,25},{17,1},{25,9},{2,18},{10... | collective-permute-start | bytes 786440 | tf_op jit(solution)/shard_map/ppermute | solution.py:84
Sparse Core Ops, SparseCore 0:
  350.3 221.8 all-reduce.1
